TPU v7x, 128 devices: a whole 4x4x4 slice. The times are simulated.
128 devices in a mesh: clip: 16 (over z_hi, y, core), frame: 8 (over x, z_lo).
Axes of the slice: x: 4, y: 4, z: 4 (z_hi: 2, z_lo: 2; z = z_hi * 2 + z_lo), core: 2. Of those that a mesh axis runs over, the one named last changes fastest.
Arguments:
- latents: bfloat16 [128, 784, 640], P(('clip', 'frame')), may hold values from -6 to 6
- timestep: int32 [128], P(('clip', 'frame')), may hold values from 0 to 999
- ref_features: bfloat16 [784, 640], P('clip'), may hold values from -6 to 6
- norm_gains: float32 [3, 640], replicated, may hold values from 0.5 to 1.5
- w_spatial: bfloat16 [4, 640, 640], replicated, as said below
- w_temporal: bfloat16 [4, 640, 640], replicated, as said below
- w_time: bfloat16 [640, 1280], replicated, may hold values from -0.25 to 0.25
- w_in: bfloat16 [640, 5120], replicated, may hold values from -0.25 to 0.25
- w_out: bfloat16 [2560, 640], replicated, may hold values from -0.125 to 0.125
Outputs:
- result: bfloat16 [128, 784, 640], P(('clip', 'frame'))
Inputs may be any that keep to these rules, and one draw needn't show every extreme that they name: `w_spatial`: query, key, value and output projections, in that order. `w_temporal`: query, key, value and output projections, in that order.
All inputs are finite; a program needn't handle non-finite values.
Results may differ from a plain program's by a relative error of at most 0.02.
Values may be sent and summed in bfloat16 or wider, within the bound.
A program may use at most 128 MiB of HBM per device.

v0:
```python
import math

import jax
import jax.numpy as jnp
from jax import lax
from jax.sharding import PartitionSpec as P

HEADS = 8
HEAD = 80
D = 640
FFH = 2560


def layer_norm(values, gain):
    mean = jnp.mean(values, axis=-1, keepdims=True)
    centered = values - mean
    variance = jnp.mean(centered * centered, axis=-1, keepdims=True)
    return centered * lax.rsqrt(variance + 1e-05) * gain


def head_attention(query, keys, values):
    rows = query.shape[0]
    count = keys.shape[0]
    split_q = query.reshape(rows, HEADS, HEAD).transpose(1, 0, 2)
    split_k = keys.reshape(count, HEADS, HEAD).transpose(1, 0, 2)
    split_v = values.reshape(count, HEADS, HEAD).transpose(1, 0, 2)
    factor = 1.0 / math.sqrt(HEAD)

    def one_head(operands):
        head_q, head_k, head_v = operands
        scores = jnp.dot(head_q, head_k.T, preferred_element_type=jnp.float32) * factor
        top = jnp.max(scores, axis=-1, keepdims=True)
        expo = jnp.exp(scores - top)
        weights = (expo / jnp.sum(expo, axis=-1, keepdims=True)).astype(jnp.bfloat16)
        return jnp.dot(weights, head_v, preferred_element_type=jnp.float32).astype(jnp.bfloat16)

    outputs = lax.map(one_head, (split_q, split_k, split_v))
    return outputs.transpose(1, 0, 2).reshape(rows, HEADS * HEAD)


def temporal_attention(query, keys, values):
    frames, rows, width = query.shape
    head_q = query.reshape(frames, rows, HEADS, HEAD)
    head_k = keys.reshape(frames, rows, HEADS, HEAD)
    head_v = values.reshape(frames, rows, HEADS, HEAD)
    scores = jnp.einsum("fnhd,gnhd->nhfg", head_q, head_k, preferred_element_type=jnp.float32) * (
        1.0 / math.sqrt(HEAD)
    )
    top = jnp.max(scores, axis=-1, keepdims=True)
    expo = jnp.exp(scores - top)
    weights = (expo / jnp.sum(expo, axis=-1, keepdims=True)).astype(jnp.bfloat16)
    mixed = jnp.einsum("nhfg,gnhd->fnhd", weights, head_v, preferred_element_type=jnp.float32)
    return mixed.astype(jnp.bfloat16).reshape(frames, rows, width)


def time_embedding(steps):
    half = D // 2
    freqs = jnp.exp(-math.log(10000.0) * jnp.arange(half, dtype=jnp.float32) / half)
    angles = steps.astype(jnp.float32)[:, None] * freqs[None, :]
    return jnp.concatenate([jnp.cos(angles), jnp.sin(angles)], axis=-1).astype(jnp.bfloat16)


def per_device(
    latents, timestep, ref_features, norm_gains, w_spatial, w_temporal, w_time, w_in, w_out
):
    frame = latents[0]
    positions = frame.shape[0]
    group_size = lax.axis_size("frame")
    w_pair = jnp.concatenate([w_spatial[1], w_spatial[2]], axis=1)
    own_kv = jnp.dot(ref_features, w_pair, preferred_element_type=jnp.float32).astype(jnp.bfloat16)
    ref_kv = lax.all_gather(own_kv, "clip", axis=0, tiled=True)
    wide = frame.astype(jnp.float32)
    normed = layer_norm(wide, norm_gains[0]).astype(jnp.bfloat16)
    query = jnp.dot(normed, w_spatial[0], preferred_element_type=jnp.float32).astype(jnp.bfloat16)
    self_kv = jnp.dot(normed, w_pair, preferred_element_type=jnp.float32).astype(jnp.bfloat16)
    joined = jnp.concatenate([self_kv, ref_kv], axis=0)
    attended = head_attention(query, joined[:, :D], joined[:, D:])
    first = (wide + jnp.dot(attended, w_spatial[3], preferred_element_type=jnp.float32)).astype(
        jnp.bfloat16
    )
    modulation = jnp.dot(time_embedding(timestep), w_time, preferred_element_type=jnp.float32)
    shift = modulation[:, :D]
    scale = modulation[:, D:]
    normed_two = (
        layer_norm(first.astype(jnp.float32), norm_gains[1]) * (1.0 + scale) + shift
    ).astype(jnp.bfloat16)
    sectioned = normed_two.reshape(1, group_size, positions // group_size, D)
    piece = lax.all_to_all(sectioned, "frame", split_axis=1, concat_axis=0, tiled=True)
    frames = piece.shape[0]
    rows = piece.shape[2]
    flat = piece.reshape(frames * rows, D)
    tq = (
        jnp.dot(flat, w_temporal[0], preferred_element_type=jnp.float32)
        .astype(jnp.bfloat16)
        .reshape(frames, rows, D)
    )
    tk = (
        jnp.dot(flat, w_temporal[1], preferred_element_type=jnp.float32)
        .astype(jnp.bfloat16)
        .reshape(frames, rows, D)
    )
    tv = (
        jnp.dot(flat, w_temporal[2], preferred_element_type=jnp.float32)
        .astype(jnp.bfloat16)
        .reshape(frames, rows, D)
    )
    mixed = temporal_attention(tq, tk, tv).reshape(frames * rows, D)
    out = jnp.dot(mixed, w_temporal[3], preferred_element_type=jnp.float32).astype(jnp.bfloat16)
    moved = out.reshape(frames, 1, rows, D)
    returned = lax.all_to_all(moved, "frame", split_axis=0, concat_axis=1, tiled=True).reshape(
        positions, D
    )
    second = (first.astype(jnp.float32) + returned.astype(jnp.float32)).astype(jnp.bfloat16)
    wide_two = second.astype(jnp.float32)
    normed_three = layer_norm(wide_two, norm_gains[2]).astype(jnp.bfloat16)
    proj = jnp.dot(normed_three, w_in, preferred_element_type=jnp.float32)
    inner = (proj[:, :FFH] * jax.nn.gelu(proj[:, FFH:], approximate=False)).astype(jnp.bfloat16)
    result = (wide_two + jnp.dot(inner, w_out, preferred_element_type=jnp.float32)).astype(
        jnp.bfloat16
    )
    return result[None]


def solution(mesh):
    placed = (
        P(("clip", "frame"), None, None),
        P(("clip", "frame")),
        P("clip", None),
        P(),
        P(),
        P(),
        P(),
        P(),
        P(),
    )
    return jax.shard_map(
        per_device,
        mesh=mesh,
        in_specs=placed,
        out_specs=P(("clip", "frame"), None, None),
        check_vma=False,
    )
```

profile of v0, /device:TPU:32, one launch (start us, length us, event | category | flops | bytes accessed | tf_op | source)
XLA Modules:
  0.0 280.6 jit_solution(3541557882282412556)
XLA Ops:
  14.5 3.6 %convolution_convert_fusion.7 = bf16[784,640]{1,0:T(8,128)(2,1)} fusion(bf16[1,784,640]{2,1,0:T(8,128)(2,1)} %param.11, f32[640]{0:T(1024)S(1)} %get-tuple-element.44, f32[784]{0:T(1024)S(1)} %add_rsqrt_fusion.2, f32[784]{0:T(1024)S(1)} %broadcast_multiply_fusion.2, bf16[4,640,640]{2,1,0:T(8,128)(2,1)} %param.15), kind=kOutput, calls=%fused_computation.98 | convolution fusion | flops 645263360 | bytes 2835072 | tf_op jit(solution)/shard_map/dot_general | solution.py:74
  22.3 4.9 %convolution_convert_fusion = bf16[784,1280]{1,0:T(8,128)(2,1)} fusion(bf16[640,640]{1,0:T(8,128)(2,1)} %copy-done.5, bf16[640,640]{1,0:T(8,128)(2,1)} %copy-done.4, bf16[1,784,640]{2,1,0:T(8,128)(2,1)} %param.11, f32[640]{0:T(1024)S(1)} %get-tuple-element.44, f32[784]{0:T(1024)S(1)} %add_rsqrt_fusion.2, f32[784]{0:T(1024)S(1)} %broadcast_multiply_fusion.2), kind=kOutput, calls=%fused_computation.42 | convolution fusion | flops 1291294720 | bytes 4657792 | tf_op jit(solution)/shard_map/dot_general | solution.py:75
  27.2 33.8 %all-gather.3.cloned.1.call-done = bf16[16,49,1280]{2,1,0:T(8,128)(2,1)} async-done(((bf16[1,49,1280]{2,1,0:T(8,128)(2,1)}), bf16[16,49,1280]{2,1,0:T(8,128)(2,1)}) %all-gather.3.cloned.1.call-update) | async-done | bytes 2007056 | tf_op jit(solution)/shard_map/all_gather | solution.py:71
  61.0 2.9 %reshape.122 = bf16[784,1280]{1,0:T(8,128)(2,1)} reshape(bf16[16,49,1280]{2,1,0:T(8,128)(2,1)} %all-gather.3.cloned.1.call-done) | data formatting | bytes 4014080
  63.9 4.5 %pad_maximum_fusion = (bf16[1568,640]{1,0:T(8,128)(2,1)}, bf16[1568,640]{1,0:T(8,128)(2,1)}) fusion(bf16[784,1280]{1,0:T(8,128)(2,1)} %reshape.122, bf16[784,1280]{1,0:T(8,128)(2,1)} %convolution_convert_fusion), kind=kLoop, calls=%fused_computation.84 | loop fusion | flops 8028160 | bytes 8028160 | tf_op jit(solution)/shard_map/concatenate | solution.py:76
  68.4 4.1 %copy.33 = bf16[1568,640]{0,1:T(8,128)(2,1)} copy(bf16[1568,640]{1,0:T(8,128)(2,1)} %get-tuple-element.62) | data formatting | bytes 4014080 | tf_op jit(solution)/shard_map/slice | solution.py:77
  72.5 4.1 %copy.32 = bf16[1568,640]{0,1:T(8,128)(2,1)} copy(bf16[1568,640]{1,0:T(8,128)(2,1)} %get-tuple-element.63) | data formatting | bytes 4014080 | tf_op jit(solution)/shard_map/slice | solution.py:77
  76.6 48.0 %while.10 = (s32[]{:T(128)}, bf16[8,784,80]{1,2,0:T(8,128)(2,1)}, bf16[8,784,80]{1,2,0:T(8,128)(2,1)}, bf16[8,1568,80]{1,2,0:T(8,128)(2,1)}, bf16[8,1568,80]{1,2,0:T(8,128)(2,1)}, /*index=5*/s32[]{:T(128)}) while((s32[]{:T(128)}, bf16[8,784,80]{1,2,0:T(8,128)(2,1)}, bf16[8,784,80]{1,2,0:T(8,128)(2,1)}, bf16[8,1568,80]{1,2,0:T(8,128)(2,1)}, ...), condition=%wide.region_5.6_spmd, body=%wide.region_2.5_spmd.sunk | while | flops 404504800 | bytes 15588749 | solution.py:37
  79.7 2.9 %fusion.151 = bf16[8,784,80]{1,2,0:T(8,128)(2,1)} fusion(bf16[8,784,80]{1,2,0:T(8,128)(2,1)} %get-tuple-element.114, s32[]{:T(128)S(6)} %copy.68, f32[784,1568]{1,0:T(8,128)S(1)} %get-tuple-element.105, f32[784]{0:T(1024)S(1)} %fusion.150, f32[784]{0:T(1024)S(1)} %get-tuple-element.106, bf16[8,1568,80]{1,2,0:T(8,128)(2,1)} %get-tuple-element.123), kind=kOutput, calls=%fused_computation.7.clone.1 | convolution fusion | flops 201669888 | bytes 5334144 | tf_op jit(solution)/shard_map/while/body/eval_jaxpr/dot_general | solution.py:35
  85.7 2.9 %fusion.151 = bf16[8,784,80]{1,2,0:T(8,128)(2,1)} fusion(bf16[8,784,80]{1,2,0:T(8,128)(2,1)} %get-tuple-element.114, s32[]{:T(128)S(6)} %copy.68, f32[784,1568]{1,0:T(8,128)S(1)} %get-tuple-element.105, f32[784]{0:T(1024)S(1)} %fusion.150, f32[784]{0:T(1024)S(1)} %get-tuple-element.106, bf16[8,1568,80]{1,2,0:T(8,128)(2,1)} %get-tuple-element.123), kind=kOutput, calls=%fused_computation.7.clone.1 | convolution fusion | flops 201669888 | bytes 5334144 | tf_op jit(solution)/shard_map/while/body/eval_jaxpr/dot_general | solution.py:35
  91.7 2.9 %fusion.151 = bf16[8,784,80]{1,2,0:T(8,128)(2,1)} fusion(bf16[8,784,80]{1,2,0:T(8,128)(2,1)} %get-tuple-element.114, s32[]{:T(128)S(6)} %copy.68, f32[784,1568]{1,0:T(8,128)S(1)} %get-tuple-element.105, f32[784]{0:T(1024)S(1)} %fusion.150, f32[784]{0:T(1024)S(1)} %get-tuple-element.106, bf16[8,1568,80]{1,2,0:T(8,128)(2,1)} %get-tuple-element.123), kind=kOutput, calls=%fused_computation.7.clone.1 | convolution fusion | flops 201669888 | bytes 5334144 | tf_op jit(solution)/shard_map/while/body/eval_jaxpr/dot_general | solution.py:35
  97.7 2.9 %fusion.151 = bf16[8,784,80]{1,2,0:T(8,128)(2,1)} fusion(bf16[8,784,80]{1,2,0:T(8,128)(2,1)} %get-tuple-element.114, s32[]{:T(128)S(6)} %copy.68, f32[784,1568]{1,0:T(8,128)S(1)} %get-tuple-element.105, f32[784]{0:T(1024)S(1)} %fusion.150, f32[784]{0:T(1024)S(1)} %get-tuple-element.106, bf16[8,1568,80]{1,2,0:T(8,128)(2,1)} %get-tuple-element.123), kind=kOutput, calls=%fused_computation.7.clone.1 | convolution fusion | flops 201669888 | bytes 5334144 | tf_op jit(solution)/shard_map/while/body/eval_jaxpr/dot_general | solution.py:35
  103.7 2.9 %fusion.151 = bf16[8,784,80]{1,2,0:T(8,128)(2,1)} fusion(bf16[8,784,80]{1,2,0:T(8,128)(2,1)} %get-tuple-element.114, s32[]{:T(128)S(6)} %copy.68, f32[784,1568]{1,0:T(8,128)S(1)} %get-tuple-element.105, f32[784]{0:T(1024)S(1)} %fusion.150, f32[784]{0:T(1024)S(1)} %get-tuple-element.106, bf16[8,1568,80]{1,2,0:T(8,128)(2,1)} %get-tuple-element.123), kind=kOutput, calls=%fused_computation.7.clone.1 | convolution fusion | flops 201669888 | bytes 5334144 | tf_op jit(solution)/shard_map/while/body/eval_jaxpr/dot_general | solution.py:35
  109.7 2.9 %fusion.151 = bf16[8,784,80]{1,2,0:T(8,128)(2,1)} fusion(bf16[8,784,80]{1,2,0:T(8,128)(2,1)} %get-tuple-element.114, s32[]{:T(128)S(6)} %copy.68, f32[784,1568]{1,0:T(8,128)S(1)} %get-tuple-element.105, f32[784]{0:T(1024)S(1)} %fusion.150, f32[784]{0:T(1024)S(1)} %get-tuple-element.106, bf16[8,1568,80]{1,2,0:T(8,128)(2,1)} %get-tuple-element.123), kind=kOutput, calls=%fused_computation.7.clone.1 | convolution fusion | flops 201669888 | bytes 5334144 | tf_op jit(solution)/shard_map/while/body/eval_jaxpr/dot_general | solution.py:35
  115.7 2.9 %fusion.151 = bf16[8,784,80]{1,2,0:T(8,128)(2,1)} fusion(bf16[8,784,80]{1,2,0:T(8,128)(2,1)} %get-tuple-element.114, s32[]{:T(128)S(6)} %copy.68, f32[784,1568]{1,0:T(8,128)S(1)} %get-tuple-element.105, f32[784]{0:T(1024)S(1)} %fusion.150, f32[784]{0:T(1024)S(1)} %get-tuple-element.106, bf16[8,1568,80]{1,2,0:T(8,128)(2,1)} %get-tuple-element.123), kind=kOutput, calls=%fused_computation.7.clone.1 | convolution fusion | flops 201669888 | bytes 5334144 | tf_op jit(solution)/shard_map/while/body/eval_jaxpr/dot_general | solution.py:35
  121.7 2.9 %fusion.151 = bf16[8,784,80]{1,2,0:T(8,128)(2,1)} fusion(bf16[8,784,80]{1,2,0:T(8,128)(2,1)} %get-tuple-element.114, s32[]{:T(128)S(6)} %copy.68, f32[784,1568]{1,0:T(8,128)S(1)} %get-tuple-element.105, f32[784]{0:T(1024)S(1)} %fusion.150, f32[784]{0:T(1024)S(1)} %get-tuple-element.106, bf16[8,1568,80]{1,2,0:T(8,128)(2,1)} %get-tuple-element.123), kind=kOutput, calls=%fused_computation.7.clone.1 | convolution fusion | flops 201669888 | bytes 5334144 | tf_op jit(solution)/shard_map/while/body/eval_jaxpr/dot_general | solution.py:35
  124.6 3.0 %convert_reduce_fusion.1 = (f32[784]{0:T(1024)S(1)}, bf16[784,640]{1,0:T(8,128)(2,1)S(1)}) fusion(bf16[784,640]{0,1:T(8,128)(2,1)} %bitcast.118, bf16[4,640,640]{2,1,0:T(8,128)(2,1)} %param.15, bf16[1,784,640]{2,1,0:T(8,128)(2,1)} %param.11), kind=kOutput, calls=%fused_computation.50 | convolution fusion | flops 644760832 | bytes 3976256 | tf_op jit(solution)/shard_map/dot_general | solution.py:78
  132.6 21.0 %all_to_all.8 = bf16[1,8,98,640]{3,2,0,1:T(8,128)(2,1)} all-to-all(bf16[1,8,98,640]{3,2,0,1:T(8,128)(2,1)} %bitcast.114), channel_id=1, replica_groups=mesh['clip'=16,'frame'=8] {'frame'}, dimensions={1} | all-to-all | bytes 2007040 | tf_op jit(solution)/shard_map/all_to_all | solution.py:88
  156.1 3.6 %convolution_convert_fusion.4 = bf16[784,640]{1,0:T(8,128)(2,1)} fusion(bf16[784,640]{1,0:T(8,128)(2,1)} %reshape.118, bf16[4,640,640]{2,1,0:T(8,128)(2,1)} %param.16), kind=kOutput, calls=%fused_computation.95 | convolution fusion | flops 642754560 | bytes 2826240 | tf_op jit(solution)/shard_map/dot_general | solution.py:98
  159.7 3.2 %convolution_convert_fusion.5 = bf16[784,640]{1,0:T(8,128)(2,1)} fusion(bf16[784,640]{1,0:T(8,128)(2,1)S(1)} %copy-done.3, bf16[4,640,640]{2,1,0:T(8,128)(2,1)} %param.16), kind=kOutput, calls=%fused_computation.96 | convolution fusion | flops 642754560 | bytes 2826240 | tf_op jit(solution)/shard_map/dot_general | solution.py:93
  162.9 3.2 %convolution_convert_fusion.6 = bf16[784,640]{1,0:T(8,128)(2,1)} fusion(bf16[784,640]{1,0:T(8,128)(2,1)S(1)} %copy-done.3, bf16[4,640,640]{2,1,0:T(8,128)(2,1)} %param.16), kind=kOutput, calls=%fused_computation.97 | convolution fusion | flops 642754560 | bytes 2826240 | tf_op jit(solution)/shard_map/dot_general | solution.py:103
  166.1 3.9 %reshape.128 = bf16[8,98,8,80]{3,2,1,0:T(8,128)(2,1)} reshape(bf16[784,640]{1,0:T(8,128)(2,1)} %convolution_convert_fusion.4) | data formatting | bytes 2007040 | tf_op jit(solution)/shard_map/reshape;reshape | solution.py:44
  170.0 4.0 %reshape.126 = bf16[8,98,8,80]{3,2,1,0:T(8,128)(2,1)} reshape(bf16[784,640]{1,0:T(8,128)(2,1)} %convolution_convert_fusion.6) | data formatting | bytes 2007040 | tf_op jit(solution)/shard_map/reshape;reshape | solution.py:45
  174.0 4.0 %reshape.127 = bf16[8,98,8,80]{3,2,1,0:T(8,128)(2,1)} reshape(bf16[784,640]{1,0:T(8,128)(2,1)} %convolution_convert_fusion.5) | data formatting | bytes 2007040 | tf_op jit(solution)/shard_map/reshape;reshape | solution.py:43
  178.0 2.9 %fusion.59 = f32[98,8,8,8]{2,3,1,0:T(8,128)S(1)} fusion(bf16[8,98,8,80]{3,2,1,0:T(8,128)(2,1)} %reshape.128, bf16[8,98,8,80]{3,2,1,0:T(8,128)(2,1)} %reshape.127), kind=kOutput, calls=%fused_computation.87 | convolution fusion | flops 8028160 | bytes 2207744 | tf_op jit(solution)/shard_map/fnhd,gnhd->nhfg/dot_general | solution.py:46
  180.8 22.5 %fusion.134 = (f32[98,8,8]{2,1,0:T(8,128)S(1)}, f32[98,8,8,8]{2,3,1,0:T(8,128)S(1)}) fusion(f32[98,8,8,8]{2,3,1,0:T(8,128)S(1)} %fusion.59), kind=kOutput, calls=%fused_computation.174 | output fusion | flops 200711 | bytes 426496 | tf_op jit(solution)/shard_map/sub | solution.py:50
  205.6 4.0 %copy.45 = bf16[8,98,8,80]{1,0,3,2:T(8,128)(2,1)} copy(bf16[8,98,8,80]{3,0,2,1:T(8,128)(2,1)} %fusion.67) | data formatting | bytes 2007040 | tf_op jit(solution)/shard_map/convert_element_type | solution.py:53
  209.6 3.5 %reshape_reshape.15 = bf16[784,640]{0,1:T(8,128)(2,1)} reshape(bf16[8,98,8,80]{1,0,3,2:T(8,128)(2,1)} %copy.45) | data formatting | bytes 2007040 | tf_op jit(solution)/shard_map/reshape;reshape | solution.py:107
  213.1 3.6 %convolution_convert_fusion.3 = bf16[784,640]{1,0:T(8,128)(2,1)} fusion(bf16[784,640]{0,1:T(8,128)(2,1)} %reshape_reshape.15, bf16[4,640,640]{2,1,0:T(8,128)(2,1)} %param.16), kind=kOutput, calls=%fused_computation.94 | convolution fusion | flops 642754560 | bytes 2969600 | tf_op jit(solution)/shard_map/dot_general | solution.py:108
  219.2 19.6 %all_to_all.9 = bf16[8,1,98,640]{3,2,1,0:T(8,128)(2,1)} all-to-all(bf16[8,1,98,640]{3,2,1,0:T(8,128)(2,1)} %bitcast.115), channel_id=1, replica_groups=mesh['clip'=16,'frame'=8] {'frame'}, dimensions={0} | all-to-all | bytes 2007040 | tf_op jit(solution)/shard_map/all_to_all | solution.py:110
  244.2 8.7 %fusion.76 = f32[784,5120]{1,0:T(8,128)S(1)} fusion(bf16[640,5120]{1,0:T(8,128)(2,1)} %param.18, bf16[784,640]{1,0:T(8,128)(2,1)S(1)} %get-tuple-element.59, f32[640]{0:T(1024)S(1)} %get-tuple-element.43, f32[784]{0:T(1024)S(1)} %add_rsqrt_fusion, f32[784]{0:T(1024)S(1)} %broadcast_multiply_fusion), kind=kOutput, calls=%fused_computation.101 | convolution fusion | flops 5140531200 | bytes 23622272 | tf_op jit(solution)/shard_map/dot_general | solution.py:116
  252.9 20.8 %fusion.70 = bf16[1,784,640]{2,1,0:T(8,128)(2,1)} fusion(bf16[2560,640]{1,0:T(8,128)(2,1)S(1)} %copy-done, f32[784,5120]{1,0:T(8,128)S(1)} %fusion.76, bf16[784,640]{1,0:T(8,128)(2,1)S(1)} %get-tuple-element.59), kind=kOutput, calls=%fused_computation.99 | convolution fusion | flops 2702981120 | bytes 21340160 | tf_op jit(solution)/shard_map/dot_general | solution.py:118
  (61 shorter events, 53.5 us)
Async XLA Ops:
  6.5 246.4 %copy-start = (bf16[2560,640]{1,0:T(8,128)(2,1)S(1)}, bf16[2560,640]{1,0:T(8,128)(2,1)}, u32[]{:S(2)}) copy-start(bf16[2560,640]{1,0:T(8,128)(2,1)} %param.19) | copy-start | bytes 9830404
  6.5 2.9 %copy-start.7 = (bf16[49,640]{1,0:T(8,128)(2,1)S(1)}, bf16[49,640]{1,0:T(8,128)(2,1)}, u32[]{:S(2)}) copy-start(bf16[49,640]{1,0:T(8,128)(2,1)} %param.13) | copy-start | bytes 188164
  6.5 4.8 %copy-start.6 = (f32[3,640]{1,0:T(4,128)S(1)}, f32[3,640]{1,0:T(4,128)}, u32[]{:S(2)}) copy-start(f32[3,640]{1,0:T(4,128)} %param.14) | copy-start | bytes 23044
  6.5 54.5 %all-gather.3.cloned.1.call-start = ((), (), s32[]{:S(2)}) async-start(), calls=%async_computation.2 | async-start | bytes 2437120 | tf_op jit(solution)/shard_map/all_gather | solution.py:71
  8.2 0.9 copy-start.4
  8.2 1.2 copy-start.5
  127.7 1.0 copy-start.1
  156.1 3.6 %copy-start.3 = (bf16[784,640]{1,0:T(8,128)(2,1)S(1)}, bf16[784,640]{1,0:T(8,128)(2,1)}, u32[]{:S(2)}) copy-start(bf16[784,640]{1,0:T(8,128)(2,1)} %reshape.118) | copy-start | bytes 3010564
  180.8 22.5 %copy-start.2 = (bf16[8,98,8,80]{3,2,1,0:T(8,128)(2,1)S(1)}, bf16[8,98,8,80]{3,2,1,0:T(8,128)(2,1)}, u32[]{:S(2)}) copy-start(bf16[8,98,8,80]{3,2,1,0:T(8,128)(2,1)} %reshape.126) | copy-start | bytes 3010564
Sparse Core Ops, SparseCore 0:
  10.6 50.3 all-gather.2
where the time goes:
time: 284 us; the launch traced here: 281 us
  matrix products  102 us (36%)
  local copies, waits for them, and re-layouts  46.5 us (16%)
  other arithmetic  43 us (15%)
  blocking collectives  40.6 us (14%)
  waiting for transfers between devices  33.9 us (12%)
  between operations  14.2 us (5%)
    all_gather x1, waiting for transfers between devices, per_device(): ref_kv = lax.all_gather(own_kv, 'clip', axis=0, tiled=True)  33.8 us
    dot_general x8, matrix products, one_head(): jnp.dot(weights, head_v, preferred_element_type=jnp.float32)  23.4 us
    sub x1, other arithmetic, temporal_attention(): expo = jnp.exp(scores - top)  22.5 us
    all_to_all x1, blocking collectives, per_device(): lax.all_to_all(sectioned, 'frame', split_axis=1, concat_axis=0, tiled=True)  21 us
    dot_general x1, matrix products, per_device(): jnp.dot(inner, w_out, preferred_element_type=jnp.float32)  20.8 us
    all_to_all x1, blocking collectives, per_device(): lax.all_to_all(moved, 'frame', split_axis=0, concat_axis=1, tiled=True)  19.6 us
    dot_general x8, matrix products, one_head(): jnp.dot(head_q, head_k.T, preferred_element_type=jnp.float32) * factor  16.4 us
    dot_general x1, matrix products, per_device(): proj = jnp.dot(normed_three, w_in, preferred_element_type=jnp.float32)  8.71 us
  transfers between devices with their start and end apart: 1, of which 1 were waited for; matrix products, arithmetic and copies ran while one was open for 6% of the time, Pallas kernels for 0%

commit v1 on v0

v1 whole, which is shorter than its diff:
```python
import math

import jax
import jax.numpy as jnp
from jax import lax
from jax.experimental import pallas as pl
from jax.experimental.pallas import tpu as pltpu
from jax.sharding import PartitionSpec as P

HEADS = 8
HEAD = 80
D = 640
FFH = 2560
ROWS = 784
PAD = 128
WIDE = HEADS * PAD
CLIP = 16
FRAME = 8
OWNERS = 7
BLOCK = 112
REF = 49
REF_PAD = 64
KEYS_SELF = 768
KEYS_REF = CLIP * REF_PAD
HALVES = ((0, 64, 0), (448, 48, 64))
LOG2E = 1.4426950408889634
FACTOR = LOG2E / math.sqrt(HEAD)
F32 = jnp.float32
BF16 = jnp.bfloat16
MESH = pl.DeviceIdType.MESH


def dot(a, b):
    return jnp.dot(a, b, preferred_element_type=F32)


def norm(wide):
    mean = jnp.mean(wide, axis=-1, keepdims=True)
    centered = wide - mean
    variance = jnp.mean(centered * centered, axis=-1, keepdims=True)
    return centered * lax.rsqrt(variance + 1e-05)


def iota(shape, axis):
    return lax.broadcasted_iota(jnp.int32, shape, axis)


def head_of(column):
    return (column * 52429) >> 22


def body(
    lat, ref, emb, gains, w_spatial, w_temporal, w_time, w_in, w_out, out,
    x, first, h, q, k_t, v, ref_stage, ref_all, kr_t, vr, acc, attn, wq, wk, wv, wo,
    ws, wt, wtime, win, wout, mod, spread, gather,
    recv_a, recv_b, tq, tk, tv, mixed, moved_a, moved_b, ret, inner, result,
    sem_x, sem_w, sem_out, ref_send, ref_recv, go_send, go_recv, back_send, back_recv,
):
    me_c = lax.axis_index("clip")
    me_f = lax.axis_index("frame")

    loads_x = []
    for half, (start, count, inside) in enumerate(HALVES):
        for j in range(OWNERS):
            loads_x.append(
                pltpu.make_async_copy(
                    lat.at[pl.ds(BLOCK * j + inside, count)],
                    x.at[pl.ds(start + count * j, count)],
                    sem_x.at[half * OWNERS + j],
                )
            )
    load_ws = pltpu.make_async_copy(w_spatial, ws, sem_w.at[0])
    load_wtime = pltpu.make_async_copy(w_time, wtime, sem_w.at[1])
    load_wt = pltpu.make_async_copy(w_temporal, wt, sem_w.at[2])
    load_win = pltpu.make_async_copy(w_in, win, sem_w.at[3])
    load_wout = pltpu.make_async_copy(w_out, wout, sem_w.at[4])
    for load in loads_x:
        load.start()
    load_ws.start()
    load_wtime.start()
    load_wt.start()
    load_win.start()
    load_wout.start()

    ref_stage[...] = jnp.zeros_like(ref_stage)
    ref_stage[0:REF, :] = ref[...]

    barrier = pltpu.get_barrier_semaphore()

    @pl.loop(1, CLIP)
    def _(d):
        pl.semaphore_signal(
            barrier, inc=1, device_id={"clip": lax.rem(me_c + d, CLIP)}, device_id_type=MESH
        )

    @pl.loop(1, FRAME)
    def _(d):
        pl.semaphore_signal(
            barrier, inc=1, device_id={"frame": lax.rem(me_f + d, FRAME)}, device_id_type=MESH
        )

    pl.semaphore_wait(barrier, CLIP + FRAME - 2)

    def ref_copy(d):
        return pltpu.make_async_remote_copy(
            src_ref=ref_stage,
            dst_ref=ref_all.at[pl.ds(pl.multiple_of(me_c * REF_PAD, REF_PAD), REF_PAD)],
            send_sem=ref_send.at[d],
            recv_sem=ref_recv.at[d],
            device_id={"clip": lax.rem(me_c + d, CLIP)},
            device_id_type=MESH,
        )

    @pl.loop(1, CLIP)
    def _(d):
        ref_copy(d).start()

    ref_all[pl.ds(pl.multiple_of(me_c * REF_PAD, REF_PAD), REF_PAD), :] = ref_stage[...]

    load_ws.wait()
    wq[...] = jnp.zeros_like(wq)
    wk[...] = jnp.zeros_like(wk)
    wv[...] = jnp.zeros_like(wv)
    wo[...] = jnp.zeros_like(wo)
    for i, target in enumerate((wq, wk, wv)):
        for n in range(HEADS):
            target[:, PAD * n : PAD * n + HEAD] = ws[i, :, HEAD * n : HEAD * n + HEAD]
    for n in range(HEADS):
        wo[PAD * n : PAD * n + HEAD, :] = ws[3, HEAD * n : HEAD * n + HEAD, :]

    for load in loads_x:
        load.wait()

    @pl.loop(0, ROWS // BLOCK)
    def _(i):
        rows = pl.ds(pl.multiple_of(i * BLOCK, BLOCK), BLOCK)
        h[rows, :] = (norm(x[rows, :].astype(F32)) * gains[0:1, :]).astype(BF16)

    @pl.loop(0, WIDE // 256)
    def _(j):
        c = pl.ds(pl.multiple_of(j * 256, 256), 256)
        lane = iota((1, 256), 1) & (PAD - 1)
        q[:, c] = jnp.where(lane == HEAD, 1.0, dot(h[...], wq[:, c]) * FACTOR).astype(BF16)
        k_t[c, :] = dot(h[0:KEYS_SELF, :], wk[:, c]).astype(BF16).T
        v[:, c] = jnp.where(lane == HEAD, 1.0, dot(h[0:KEYS_SELF, :], wv[:, c])).astype(BF16)

    @pl.loop(0, HEADS)
    def _(n):
        c = pl.ds(pl.multiple_of(n * PAD, PAD), PAD)
        s = dot(q[:, c], k_t[c, :])
        top = jnp.max(s, axis=1, keepdims=True)
        o = dot(jnp.exp2(s - top).astype(BF16), v[:, c])
        acc[:, c] = jnp.where(iota((1, PAD), 1) == HEAD + 1, top, o)

    load_wtime.wait()
    mod[...] = dot(emb[...], wtime[...])

    @pl.loop(0, FRAME)
    def _(g):
        lane = iota((D, PAD), 1) & (HEADS * FRAME - 1)
        gather[g] = (lane == FRAME * g + head_of(iota((D, PAD), 0))).astype(F32).astype(BF16)
        spread[g] = (
            (iota((PAD, D), 0) == FRAME * g + head_of(iota((PAD, D), 1))).astype(F32).astype(BF16)
        )

    @pl.loop(1, CLIP)
    def _(d):
        ref_copy(d).wait_recv()

    row = iota((PAD, 16), 0)
    tail = iota((PAD, 16), 1)
    place = ((row < REF_PAD) & (row == tail + REF)) | ((row == REF_PAD + REF) & (tail == 15))
    placed = dot(place.astype(F32).astype(BF16), h[KEYS_SELF:ROWS, :])
    ref_all[0:PAD, :] = (ref_all[0:PAD, :].astype(F32) + placed).astype(BF16)

    @pl.loop(0, WIDE // 256)
    def _(j):
        c = pl.ds(pl.multiple_of(j * 256, 256), 256)
        lane = iota((1, 256), 1) & (PAD - 1)
        key = iota((KEYS_REF, 1), 0)
        valid = ((key & (REF_PAD - 1)) < REF) | (key < REF_PAD) | (key == REF_PAD + REF)
        mask = jnp.where(valid, 0.0, -1e30)
        kr_t[c, :] = jnp.where(lane == HEAD, mask, dot(ref_all[...], wk[:, c])).astype(BF16).T
        vr[:, c] = jnp.where(lane == HEAD, 1.0, dot(ref_all[...], wv[:, c])).astype(BF16)

    def go_copy(half, d):
        start, count, _ = HALVES[half]
        target = lax.rem(me_f + d, FRAME)
        block = lax.min(target, OWNERS - 1)
        return pltpu.make_async_remote_copy(
            src_ref=h.at[pl.ds(pl.multiple_of(start + block * count, 16), count)],
            dst_ref=(recv_a, recv_b)[half].at[me_f],
            send_sem=go_send.at[half * FRAME + d],
            recv_sem=go_recv.at[half * FRAME + d],
            device_id={"frame": target},
            device_id_type=MESH,
        )

    def is_owner(d):
        return lax.rem(me_f + d, FRAME) < OWNERS

    def comes_from_owner(d):
        return lax.rem(me_f + FRAME - d, FRAME) < OWNERS

    for half, (start, count, _) in enumerate(HALVES):
        size = count * OWNERS
        rows = pl.ds(start, size)

        @pl.loop(0, HEADS)
        def _(n):
            c = pl.ds(pl.multiple_of(n * PAD, PAD), PAD)
            s = dot(q[rows, c], kr_t[c, :])
            top_r = jnp.max(s, axis=1, keepdims=True)
            o_r = dot(jnp.exp2(s - top_r).astype(BF16), vr[:, c])
            o_s = acc[rows, c]
            top_s = o_s[:, HEAD + 1 : HEAD + 2]
            top = jnp.maximum(top_r, top_s)
            o = o_s * jnp.exp2(top_s - top) + o_r * jnp.exp2(top_r - top)
            attn[0:size, c] = (o / o[:, HEAD : HEAD + 1]).astype(BF16)

        for c0, c1 in ((0, 256), (256, 512), (512, D)):
            first[rows, c0:c1] = (
                x[rows, c0:c1].astype(F32) + dot(attn[0:size, :], wo[:, c0:c1])
            ).astype(BF16)

        @pl.loop(0, OWNERS)
        def _(i):
            part = pl.ds(pl.multiple_of(start + i * count, 16), count)
            normed = norm(first[part, :].astype(F32)) * gains[1:2, :]
            h[part, :] = (normed * (1.0 + mod[0:1, D:]) + mod[0:1, :D]).astype(BF16)

        @pl.loop(1, FRAME)
        def _(d):
            @pl.when(is_owner(d))
            def _():
                go_copy(half, d).start()

        @pl.when(me_f < OWNERS)
        def _():
            (recv_a, recv_b)[half][me_f] = h[
                pl.ds(pl.multiple_of(start + lax.min(me_f, OWNERS - 1) * count, 16), count), :
            ]

    def back_copy(half, d):
        start, count, _ = HALVES[half]
        target = lax.rem(me_f + d, FRAME)
        return pltpu.make_async_remote_copy(
            src_ref=(moved_a, moved_b)[half].at[target],
            dst_ref=ret.at[pl.ds(pl.multiple_of(start + lax.min(me_f, OWNERS - 1) * count, 16), count)],
            send_sem=back_send.at[half * FRAME + d],
            recv_sem=back_recv.at[half * FRAME + d],
            device_id={"frame": target},
            device_id_type=MESH,
        )

    load_wt.wait()

    @pl.when(me_f < OWNERS)
    def _():
        for half, (start, count, _) in enumerate(HALVES):
            size = count * FRAME
            recv = (recv_a, recv_b)[half]
            moved = (moved_a, moved_b)[half]

            @pl.loop(1, FRAME)
            def _(d):
                go_copy(half, d).wait_recv()

            for c0, c1 in ((0, 256), (256, 512), (512, D)):
                states = recv[...].reshape(size, D)
                tq[0:size, c0:c1] = (dot(states, wt[0, :, c0:c1]) * FACTOR).astype(BF16)
                tk[0:size, c0:c1] = dot(states, wt[1, :, c0:c1]).astype(BF16)
                tv[0:size, c0:c1] = dot(states, wt[2, :, c0:c1]).astype(BF16)

            s = jnp.zeros((size, PAD), F32)
            for g in range(FRAME):
                keys = tk[g * count : (g + 1) * count, :]
                pairs = tq[0:size, :].reshape(FRAME, count, D) * keys[None]
                s = s + dot(pairs.reshape(size, D), gather[g])
            top = s
            for shift in (8, 16, 32):
                top = jnp.maximum(top, pltpu.roll(top, shift, 1))
            e = jnp.exp2(s - top)
            total = e
            for shift in (8, 16, 32):
                total = total + pltpu.roll(total, shift, 1)
            weights = (e / total).astype(BF16)
            for c0, c1 in ((0, 256), (256, 512), (512, D)):
                sums = jnp.zeros((FRAME, count, c1 - c0), F32)
                for g in range(FRAME):
                    values = tv[g * count : (g + 1) * count, c0:c1].astype(F32)
                    wide = dot(weights, spread[g, :, c0:c1]).reshape(FRAME, count, c1 - c0)
                    sums = sums + wide * values[None]
                mixed[0:size, c0:c1] = sums.reshape(size, c1 - c0).astype(BF16)
            for c0, c1 in ((0, 256), (256, 512), (512, D)):
                moved[:, :, c0:c1] = (
                    dot(mixed[0:size, :], wt[3, :, c0:c1]).astype(BF16).reshape(FRAME, count, c1 - c0)
                )

            @pl.loop(1, FRAME)
            def _(d):
                back_copy(half, d).start()

            ret[pl.ds(pl.multiple_of(start + lax.min(me_f, OWNERS - 1) * count, 16), count), :] = moved[
                me_f
            ]

    load_win.wait()
    load_wout.wait()
    stores = []
    for half, (start, count, inside) in enumerate(HALVES):
        size = count * OWNERS
        rows = pl.ds(start, size)

        @pl.loop(1, FRAME)
        def _(d):
            @pl.when(comes_from_owner(d))
            def _():
                back_copy(half, d).wait_recv()

        @pl.loop(0, OWNERS)
        def _(i):
            part = pl.ds(pl.multiple_of(start + i * count, 16), count)
            second = (first[part, :].astype(F32) + ret[part, :].astype(F32)).astype(BF16)
            x[part, :] = second
            first[part, :] = (norm(second.astype(F32)) * gains[2:3, :]).astype(BF16)

        @pl.loop(0, FFH // 256)
        def _(j):
            c = pl.ds(pl.multiple_of(j * 256, 256), 256)
            g = pl.ds(pl.multiple_of(FFH + j * 256, 256), 256)
            value = dot(first[rows, :], win[:, c])
            gate = dot(first[rows, :], win[:, g])
            gelu = 0.5 * gate * (1.0 + lax.erf(gate * (1.0 / math.sqrt(2.0))))
            inner[0:size, c] = (value * gelu).astype(BF16)

        for c0, c1 in ((0, 256), (256, 512), (512, D)):
            result[rows, c0:c1] = (
                x[rows, c0:c1].astype(F32) + dot(inner[0:size, :], wout[:, c0:c1])
            ).astype(BF16)
        for j in range(OWNERS):
            store = pltpu.make_async_copy(
                result.at[pl.ds(start + count * j, count)],
                out.at[pl.ds(BLOCK * j + inside, count)],
                sem_out.at[half * OWNERS + j],
            )
            store.start()
            stores.append(store)

    @pl.loop(1, CLIP)
    def _(d):
        ref_copy(d).wait_send()

    for half in range(2):

        @pl.loop(1, FRAME)
        def _(d):
            @pl.when(is_owner(d))
            def _():
                go_copy(half, d).wait_send()

            @pl.when(me_f < OWNERS)
            def _():
                back_copy(half, d).wait_send()

    for store in stores:
        store.wait()


def time_embedding(steps):
    half = D // 2
    freqs = jnp.exp(-math.log(10000.0) * jnp.arange(half, dtype=F32) / half)
    angles = steps.astype(F32)[:, None] * freqs[None, :]
    return jnp.concatenate([jnp.cos(angles), jnp.sin(angles)], axis=-1).astype(BF16)


def per_device(
    latents, timestep, ref_features, norm_gains, w_spatial, w_temporal, w_time, w_in, w_out
):
    emb = jnp.broadcast_to(time_embedding(timestep), (16, D))
    vmem = pl.BlockSpec(memory_space=pltpu.VMEM)
    hbm = pl.BlockSpec(memory_space=pl.ANY)
    sems = pltpu.SemaphoreType.DMA
    result = pl.pallas_call(
        body,
        out_shape=jax.ShapeDtypeStruct((ROWS, D), BF16),
        in_specs=[hbm, vmem, vmem, vmem, hbm, hbm, hbm, hbm, hbm],
        out_specs=hbm,
        scratch_shapes=[
            pltpu.VMEM((ROWS, D), BF16),
            pltpu.VMEM((ROWS, D), BF16),
            pltpu.VMEM((ROWS, D), BF16),
            pltpu.VMEM((ROWS, WIDE), BF16),
            pltpu.VMEM((WIDE, KEYS_SELF), BF16),
            pltpu.VMEM((KEYS_SELF, WIDE), BF16),
            pltpu.VMEM((REF_PAD, D), BF16),
            pltpu.VMEM((KEYS_REF, D), BF16),
            pltpu.VMEM((WIDE, KEYS_REF), BF16),
            pltpu.VMEM((KEYS_REF, WIDE), BF16),
            pltpu.VMEM((ROWS, WIDE), F32),
            pltpu.VMEM((448, WIDE), BF16),
            pltpu.VMEM((D, WIDE), BF16),
            pltpu.VMEM((D, WIDE), BF16),
            pltpu.VMEM((D, WIDE), BF16),
            pltpu.VMEM((WIDE, D), BF16),
            pltpu.VMEM((4, D, D), BF16),
            pltpu.VMEM((4, D, D), BF16),
            pltpu.VMEM((D, 2 * D), BF16),
            pltpu.VMEM((D, 2 * FFH), BF16),
            pltpu.VMEM((FFH, D), BF16),
            pltpu.VMEM((16, 2 * D), F32),
            pltpu.VMEM((FRAME, PAD, D), BF16),
            pltpu.VMEM((FRAME, D, PAD), BF16),
            pltpu.VMEM((FRAME, 64, D), BF16),
            pltpu.VMEM((FRAME, 48, D), BF16),
            pltpu.VMEM((512, D), BF16),
            pltpu.VMEM((512, D), BF16),
            pltpu.VMEM((512, D), BF16),
            pltpu.VMEM((512, D), BF16),
            pltpu.VMEM((FRAME, 64, D), BF16),
            pltpu.VMEM((FRAME, 48, D), BF16),
            pltpu.VMEM((ROWS, D), BF16),
            pltpu.VMEM((448, FFH), BF16),
            pltpu.VMEM((ROWS, D), BF16),
            sems((2 * OWNERS,)),
            sems((5,)),
            sems((2 * OWNERS,)),
            sems((CLIP,)),
            sems((CLIP,)),
            sems((2 * FRAME,)),
            sems((2 * FRAME,)),
            sems((2 * FRAME,)),
            sems((2 * FRAME,)),
        ],
        compiler_params=pltpu.CompilerParams(
            collective_id=0, has_side_effects=True, vmem_limit_bytes=60 * 1024 * 1024
        ),
        name="block",
    )(latents[0], ref_features, emb, norm_gains, w_spatial, w_temporal, w_time, w_in, w_out)
    return result[None]


def solution(mesh):
    placed = (
        P(("clip", "frame"), None, None),
        P(("clip", "frame")),
        P("clip", None),
        P(),
        P(),
        P(),
        P(),
        P(),
        P(),
    )
    return jax.shard_map(
        per_device,
        mesh=mesh,
        in_specs=placed,
        out_specs=P(("clip", "frame"), None, None),
        check_vma=False,
    )
```

time: 284 us -> 92.4 us (0.33); the launches traced: 281 us -> 92 us
  matrix products: 102 us -> 0 us
  Pallas kernels: 0 us -> 88.3 us
  local copies, waits for them, and re-layouts: 46.5 us -> 2.87 us
  other arithmetic: 43 us -> 0.13 us
  blocking collectives: 40.6 us -> 0 us
  waiting for transfers between devices: 33.9 us -> 0 us
  between operations: 14.2 us -> 0.67 us
    dot_general x29 -> x0, matrix products: 102 us -> none  [the longest x8 23.4 us: one_head(): jnp.dot(weights, head_v, preferred_element_type=jnp.float32)]
    pallas_call x0 -> x1, Pallas kernels: none -> 88.3 us  [per_device(): pl.pallas_call(body, out_shape=jax.ShapeDtypeStruct((ROWS, D), BF16), in_...]
    all_to_all x2 -> x0, blocking collectives: 40.6 us -> none  [the longest x1 21 us: per_device(): lax.all_to_all(sectioned, 'frame', split_axis=1, concat_axis=0, tiled=True)]
    all_gather x1 -> x0, waiting for transfers between devices: 33.8 us -> none  [per_device(): ref_kv = lax.all_gather(own_kv, 'clip', axis=0, tiled=True)]
    sub x1 -> x0, other arithmetic: 22.5 us -> none  [temporal_attention(): expo = jnp.exp(scores - top)]
    another operation x4 -> x0, local copies, waits for them, and re-layouts: 15.4 us -> none  [the longest x1 3.96 us: temporal_attention(): head_v = values.reshape(frames, rows, HEADS, HEAD)]
    reduce_sum x13 -> x0, other arithmetic: 14.3 us -> none  [the longest x8 8.09 us: one_head(): jnp.sum(expo, axis=-1, keepdims=True)]
    convert_element_type x3 -> x0, local copies, waits for them, and re-layouts: 9.23 us -> none  [the longest x1 4.04 us: temporal_attention(): return mixed.astype(jnp.bfloat16).reshape(frames, rows, width)]
  transfers between devices with their start and end apart: 1 -> 0, of which waited for: 1 -> 0; matrix products, arithmetic and copies ran while one was open for 6% -> 0% of each run, Pallas kernels for 0% -> 0%
where the time goes in v1:
time: 92.4 us; the launch traced here: 92 us
  Pallas kernels  88.3 us (96%)
  local copies, waits for them, and re-layouts  2.87 us (3%)
    pallas_call x1, Pallas kernels, per_device(): pl.pallas_call(body, out_shape=jax.ShapeDtypeStruct((ROWS, D), BF16), in_...  88.3 us
    unnamed x1, local copies, waits for them, and re-layouts  2.25 us

profile of v1, /device:TPU:32, one launch (start us, length us, event | category | flops | bytes accessed | tf_op | source)
XLA Modules:
  0.0 92.0 jit_solution(6761553927523408762)
XLA Ops:
  0.7 0.1 sine_convert_fusion
  0.7 0.1 pad_maximum_fusion
  0.8 0.6 broadcast_in_dim.4.emb
  1.4 88.3 %block.1 = bf16[784,640]{1,0:T(8,128)(2,1)} custom-call(bf16[784,640]{1,0:T(8,128)(2,1)} %bitcast.4, bf16[49,640]{1,0:T(8,128)(2,1)} %ref.1, bf16[16,640]{1,0:T(8,128)(2,1)} %broadcast_in_dim.4.emb, f32[3,640]{1,0:T(4,128)} %gains.1, bf16[4,640,640]{2,1,0:T(8,128)(2,1)} %w_spatial.1, bf16[4,640,640]{2,1,0:T(8,128)(2,1)} %w_temporal.1, ...), custom_call_target="tpu_custom_call" | custom-call | tf_op jit(solution)/shard_map/block/pallas_call | solution.py:384
  89.8 2.2 %copy.12 = bf16[1,784,640]{2,1,0:T(8,128)(2,1)} copy(bf16[1,784,640]{2,1,0:T(8,128)(2,1)} %bitcast.3) | data formatting | bytes 2007040
